TPU v7x, 32 devices: a whole 2x2x4 slice. The times are simulated.
32 devices in a mesh: stream: 8 (over y, x, core), cross: 4 (over z).
Axes of the slice: x: 2, y: 2, z: 4, core: 2. Of those that a mesh axis runs over, the one named last changes fastest.
Arguments:
- initial_state: float32 [5, 64, 32768], P(None, 'stream', 'cross'), may hold values from -6 to 6
- forcing: float32 [5, 64, 32768], P(None, 'stream', 'cross'), may hold values from -0.3 to 0.3
- block_inverse: float32 [5, 5, 64, 32768], P(None, None, 'stream', 'cross'), may hold values from -1 to 1, as said below
- lower_decay: float32 [5, 64, 32768], P(None, 'stream', 'cross'), may hold values from 0 to 1
- upper_decay: float32 [5, 64, 32768], P(None, 'stream', 'cross'), may hold values from 0 to 1
- cross_coupling: float32 [64, 32768], P('stream', 'cross'), may hold values from 0.002 to 0.02
- iblank: int32 [64, 32768], P('stream', 'cross'), may hold values 0 or 1
- donor_receiver: int32 [1024, 1], P(('stream', 'cross')), may hold values from 0 to 31; in each aligned block of 32 rows (0 to 31, 32 to 63, ...) at most 2 rows name the same one
- donor_block: int32 [1024], P(('stream', 'cross')), may hold values from 0 to 511
- stencil_offset: int32 [1024], P(('stream', 'cross')), may hold values from 1 to 127
- stencil_weight: float32 [1024, 128], P(('stream', 'cross')), may hold values from 0.005 to 0.02
- fringe_target: int32 [2048], P(('stream', 'cross')), may hold values from 0 to 511
Outputs:
- final_state: float32 [5, 64, 32768], P(None, 'stream', 'cross')
- last_update: float32 [5, 64, 32768], P(None, 'stream', 'cross')
Inputs may be any that keep to these rules, and one draw needn't show every extreme that they name: `donor_receiver`: within the rows of one device no receiving device is named more than 2 times. `block_inverse`: each 5 x 5 block is orthogonal and symmetric.
All inputs are finite; a program needn't handle non-finite values. No bound on the sum of `iblank` on one device may be relied on, other than what follows from the above.
Results may differ from a plain program's by a relative error of at most 0.00018.
Values sent between devices are 32-bit elements; how exact they have to be, the bound alone decides.
A program may use at most 128 MiB of HBM per device.

v0:
```python
import jax
import jax.numpy as jnp
from jax import lax
from jax.sharding import PartitionSpec as P

ITERS = 2
CAP = 2


def padded_2(cells, sides, width):
    for axis, dim in sides:
        count = lax.axis_size(axis)
        head = lax.slice_in_dim(cells, 0, width, axis=dim)
        tail = lax.slice_in_dim(cells, cells.shape[dim] - width, cells.shape[dim], axis=dim)
        cells = jnp.concatenate(
            [
                lax.ppermute(tail, axis, [(i, (i + 1) % count) for i in range(count)]),
                cells,
                lax.ppermute(head, axis, [((i + 1) % count, i) for i in range(count)]),
            ],
            axis=dim,
        )
    return cells


def passed_along(value, axis, steps):
    count = lax.axis_size(axis)
    initial, last = (max(0, -steps), min(count, count - steps))
    return lax.ppermute(value, axis, [(source, source + steps) for source in range(initial, last)])


def apply_block(block_inv, vector):
    return jnp.sum(block_inv * vector[None], axis=1)


def multiply_maps(left, right):
    return jnp.sum(left[:, :, None, :] * right[None], axis=1)


def plane_of(array, index, axis):
    return lax.dynamic_index_in_dim(array, index, axis, keepdims=False)


def compose_down(driving_term, block_inv, decay):
    count = driving_term.shape[1]
    cells = driving_term.shape[2]
    identity = jnp.broadcast_to(jnp.eye(5, dtype=jnp.float32)[:, :, None], (5, 5, cells))

    def step(index, carry):
        matrix, offset = carry
        inverse = plane_of(block_inv, index, 2)
        factor = plane_of(decay, index, 1)
        matrix = multiply_maps(inverse, factor[:, None, :] * matrix)
        offset = apply_block(inverse, plane_of(driving_term, index, 1) + factor * offset)
        return (matrix, offset)

    return lax.fori_loop(0, count, step, (identity, jnp.zeros((5, cells), jnp.float32)))


def compose_up(near, block_inv, decay):
    count = near.shape[1]
    cells = near.shape[2]
    identity = jnp.broadcast_to(jnp.eye(5, dtype=jnp.float32)[:, :, None], (5, 5, cells))

    def step(turn, carry):
        matrix, offset = carry
        index = count - 1 - turn
        inverse = plane_of(block_inv, index, 2)
        factor = plane_of(decay, index, 1)
        matrix = multiply_maps(inverse, factor[:, None, :] * matrix)
        offset = plane_of(near, index, 1) + apply_block(inverse, factor * offset)
        return (matrix, offset)

    return lax.fori_loop(0, count, step, (identity, jnp.zeros((5, cells), jnp.float32)))


def sweep_down(driving_term, block_inv, decay, incoming):
    count = driving_term.shape[1]

    def step(index, carry):
        face, sweep_output = carry
        face = apply_block(
            plane_of(block_inv, index, 2),
            plane_of(driving_term, index, 1) + plane_of(decay, index, 1) * face,
        )
        return (face, lax.dynamic_update_index_in_dim(sweep_output, face, index, 1))

    return lax.fori_loop(0, count, step, (incoming, jnp.zeros_like(driving_term)))[1]


def sweep_up(near, block_inv, decay, incoming):
    count = near.shape[1]

    def step(turn, carry):
        face, sweep_output = carry
        index = count - 1 - turn
        face = plane_of(near, index, 1) + apply_block(
            plane_of(block_inv, index, 2), plane_of(decay, index, 1) * face
        )
        return (face, lax.dynamic_update_index_in_dim(sweep_output, face, index, 1))

    return lax.fori_loop(0, count, step, (incoming, jnp.zeros_like(near)))[1]


def shards(
    initial_state,
    forcing,
    block_inverse,
    lower_decay,
    upper_decay,
    cross_coupling,
    iblank,
    donor_receiver,
    donor_block,
    stencil_offset,
    stencil_weight,
    fringe_target,
):
    stream_count = lax.axis_size("stream")
    cross_count = lax.axis_size("cross")
    devices = stream_count * cross_count
    planes = initial_state.shape[1]
    cells = initial_state.shape[2]
    block_count = planes * cells // 128
    senders = donor_block.shape[0]
    hole = (1 - iblank).astype(jnp.float32)
    receiver = donor_receiver[:, 0]
    order = lax.broadcasted_iota(jnp.int32, (senders, senders), 1)
    earlier = order < order.T
    same = receiver[:, None] == receiver[None, :]
    slot_rank = jnp.sum((same & earlier).astype(jnp.int32), axis=1)
    destination = receiver * CAP + slot_rank
    block_ids = lax.broadcasted_iota(jnp.int32, (senders, block_count), 1)
    pick_table = (donor_block[:, None] == block_ids).astype(jnp.float32)
    source_lane = lax.broadcasted_iota(jnp.int32, (senders, 128, 128), 1)
    target_lane = lax.broadcasted_iota(jnp.int32, (senders, 128, 128), 2)
    offset_lookup = (source_lane == (target_lane + stencil_offset[:, None, None]) % 128).astype(
        jnp.float32
    )
    slot_ids = lax.broadcasted_iota(jnp.int32, (devices * CAP, senders), 0)
    place_table = (destination[None, :] == slot_ids).astype(jnp.float32)
    column_entries = lax.broadcasted_iota(jnp.int32, (block_count, devices * CAP), 0)
    onehot = (fringe_target[None, :] == column_entries).astype(jnp.float32)
    blank_face = jnp.zeros((5, cells), jnp.float32)
    state = initial_state
    update = jnp.zeros_like(initial_state)
    for relaxation_round in range(ITERS):
        padded = padded_2(state, (("cross", 2),), 1)
        laplace = 2.0 * state - padded[:, :, :-2] - padded[:, :, 2:]
        blocks_local = state.reshape(5, block_count, 128)
        selected_values = jnp.einsum(
            "eb,vbp->vep", pick_table, blocks_local, precision=lax.Precision.HIGHEST
        )
        displaced_values = jnp.einsum(
            "mub,ubh->muh", selected_values, offset_lookup, precision=lax.Precision.HIGHEST
        )
        values = stencil_weight[None] * (selected_values + displaced_values)
        outgoing = jnp.einsum("se,vep->vsp", place_table, values, precision=lax.Precision.HIGHEST)
        received = lax.all_to_all(
            outgoing, ("stream", "cross"), split_axis=1, concat_axis=1, tiled=True
        )
        fringe = jnp.einsum(
            "bs,vsp->vbp", onehot, received, precision=lax.Precision.HIGHEST
        ).reshape(state.shape)
        driving_term = forcing - cross_coupling[None] * laplace + hole[None] * fringe
        matrix_down, offset_down = compose_down(driving_term, block_inverse, lower_decay)

        def pass_down(turn, carry):
            face, incoming = carry
            incoming = passed_along(face, "stream", 1)
            return (apply_block(matrix_down, incoming) + offset_down, incoming)

        incoming_down = lax.fori_loop(0, stream_count, pass_down, (offset_down, blank_face))[1]
        near = sweep_down(driving_term, block_inverse, lower_decay, incoming_down)
        matrix_up, offset_up = compose_up(near, block_inverse, upper_decay)

        def pass_up(turn, carry):
            face, incoming = carry
            incoming = passed_along(face, "stream", -1)
            return (apply_block(matrix_up, incoming) + offset_up, incoming)

        incoming_up = lax.fori_loop(0, stream_count, pass_up, (offset_up, blank_face))[1]
        update = sweep_up(near, block_inverse, upper_decay, incoming_up)
        state = state + update
    return (state, update)


def solution(mesh):
    return jax.shard_map(
        shards,
        mesh=mesh,
        in_specs=(
            P(None, "stream", "cross"),
            P(None, "stream", "cross"),
            P(None, None, "stream", "cross"),
            P(None, "stream", "cross"),
            P(None, "stream", "cross"),
            P("stream", "cross"),
            P("stream", "cross"),
            P(("stream", "cross"), None),
            P(("stream", "cross")),
            P(("stream", "cross")),
            P(("stream", "cross"), None),
            P(("stream", "cross")),
        ),
        out_specs=(P(None, "stream", "cross"), P(None, "stream", "cross")),
        check_vma=False,
    )
```

profile of v0, /device:TPU:3, one launch (start us, length us, event | category | flops | bytes accessed | tf_op | source)
XLA Modules:
  0.0 806.4 jit_solution(11326317212507014265)
XLA Ops:
  5.4 6.5 all-to-all-start
  15.9 11.0 %copy.72 = f32[5,5,8,8192]{3,1,0,2:T(8,128)} copy(f32[5,5,8,8192]{3,2,1,0:T(8,128)} %param.38) | data formatting | bytes 13107200
  44.0 36.2 %while.178 = (s32[]{:T(128)}, f32[5,5,8192]{2,1,0:T(8,128)S(1)}, f32[5,8192]{1,0:T(8,128)}, f32[5,5,8,8192]{3,1,0,2:T(8,128)}, f32[5,8,8192]{2,0,1:T(8,128)S(1)}, /*index=5*/f32[5,8,8192]{2,0,1:T(8,128)}, s32[]{:T(128)}) while((s32[]{:T(128)}, f32[5,5,8192]{2,1,0:T(8,128)S(1)}, f32[5,8192]{1,0:T(8,128)}, f32[5,5,8,8192]{3,1,0,2:T(8,128)}, ...), condition=%wide.region_4.5_spmd, body=%wide.region_1.4_spmd.sunk | while | flops 2498562 | bytes 7209049 | solution.py:57
  82.8 79.5 %while.179 = (s32[]{:T(128)}, f32[5,8192]{1,0:T(8,128)}, f32[5,8192]{1,0:T(8,128)}, f32[5,5,8192]{2,1,0:T(8,128)S(1)}, f32[5,8192]{1,0:T(8,128)}, /*index=5*/s32[]{:T(128)}) while((s32[]{:T(128)}, f32[5,8192]{1,0:T(8,128)}, f32[5,8192]{1,0:T(8,128)}, f32[5,5,8192]{2,1,0:T(8,128)S(1)}, f32[5,8192]{1,0:T(8,128)}, /*index=5*/s32[]{:T(128)}) %tuple.350), condition=%wide.region_7.8_spmd, body=%wide.region_5.7_spmd.sunk | while | flops 409602 | bytes 3604645 | solution.py:173
  82.8 4.0 collective-permute-start
  91.6 5.3 collective-permute-start
  101.7 5.3 collective-permute-start
  111.8 5.3 collective-permute-start
  121.9 5.3 collective-permute-start
  132.0 5.3 collective-permute-start
  142.1 5.3 collective-permute-start
  152.2 5.3 collective-permute-start
  163.3 54.0 %while.180 = (s32[]{:T(128)}, f32[5,8192]{1,0:T(8,128)S(1)}, f32[5,8,8192]{2,1,0:T(8,128)S(1)}, f32[5,5,8,8192]{3,2,1,0:T(8,128)}, f32[5,8,8192]{2,0,1:T(8,128)}...) while((s32[]{:T(128)}, f32[5,8192]{1,0:T(8,128)S(1)}, f32[5,8,8192]{2,1,0:T(8,128)S(1)}, ...), condition=%wide.region_10.11_spmd, body=%wide.region_8.10_spmd.sunk | while | flops 450562 | bytes 4096097 | solution.py:88
  164.4 3.6 constant_dynamic-slice_fusion.16
  171.1 3.6 constant_dynamic-slice_fusion.16
  177.9 3.6 constant_dynamic-slice_fusion.16
  184.6 3.6 constant_dynamic-slice_fusion.16
  198.1 3.6 constant_dynamic-slice_fusion.16
  204.9 3.6 constant_dynamic-slice_fusion.16
  211.6 3.6 constant_dynamic-slice_fusion.16
  218.2 31.9 %while.188 = (s32[]{:T(128)}, f32[5,5,8192]{2,1,0:T(8,128)S(1)}, f32[5,8192]{1,0:T(8,128)S(1)}, f32[5,5,8,8192]{3,1,0,2:T(8,128)}, f32[5,8,8192]{2,0,1:T(8,128)}...) while((s32[]{:T(128)}, f32[5,5,8192]{2,1,0:T(8,128)S(1)}, ...), condition=%wide.region_14.15_spmd.clone, body=%wide.region_11.14_spmd.clone.sunk | while | flops 2539527 | bytes 7700649 | solution.py:74
  251.5 80.3 %while.181 = (s32[]{:T(128)}, f32[5,8192]{1,0:T(8,128)}, f32[5,8192]{1,0:T(8,128)}, f32[5,5,8192]{2,1,0:T(8,128)S(1)}, f32[5,8192]{1,0:T(8,128)S(1)}, /*index=5*/s32[]{:T(128)}) while((s32[]{:T(128)}, f32[5,8192]{1,0:T(8,128)}, f32[5,8192]{1,0:T(8,128)}, f32[5,5,8192]{2,1,0:T(8,128)S(1)}, f32[5,8192]{1,0:T(8,128)S(1)}, ...), condition=%wide.region_17.18_spmd, body=%wide.region_15.17_spmd.sunk | while | flops 409602 | bytes 2949257 | solution.py:182
  253.5 7.5 collective-permute-done.1
  264.1 6.9 collective-permute-done.1
  274.0 6.9 collective-permute-done.1
  284.0 6.9 collective-permute-done.1
  293.9 6.9 collective-permute-done.1
  303.9 6.9 collective-permute-done.1
  313.8 6.9 collective-permute-done.1
  323.8 6.9 collective-permute-done.1
  333.0 82.2 %while.182 = (s32[]{:T(128)}, f32[5,8192]{1,0:T(8,128)S(1)}, f32[5,8,8192]{2,1,0:T(8,128)}, f32[5,8,8192]{2,1,0:T(8,128)S(1)}, f32[5,5,8,8192]{3,2,1,0:T(8,128)}...) while((s32[]{:T(128)}, f32[5,8192]{1,0:T(8,128)S(1)}, ...), condition=%wide.region_20.21_spmd, body=%wide.region_18.20_spmd.sunk | while | flops 491526 | bytes 4751523 | solution.py:102
  333.0 3.7 constant_dynamic-slice_fusion.17
  339.0 4.2 dynamic_update_slice.41
  349.3 4.2 dynamic_update_slice.41
  359.5 4.2 dynamic_update_slice.41
  369.8 4.2 dynamic_update_slice.41
  380.0 4.2 dynamic_update_slice.41
  390.3 4.2 dynamic_update_slice.41
  400.6 4.2 dynamic_update_slice.41
  410.8 4.2 dynamic_update_slice.41
  426.0 6.9 all-to-all-done.1
  441.1 38.1 %while.183 = (s32[]{:T(128)}, f32[5,5,8192]{2,1,0:T(8,128)S(1)}, f32[5,8192]{1,0:T(8,128)S(1)}, f32[5,5,8,8192]{3,1,0,2:T(8,128)}, f32[5,8,8192]{2,0,1:T(8,128)}, /*index=5*/f32[5,8,8192]{2,0,1:T(8,128)}, s32[]{:T(128)}) while((s32[]{:T(128)}, f32[5,5,8192]{2,1,0:T(8,128)S(1)}, f32[5,8192]{1,0:T(8,128)S(1)}, f32[5,5,8,8192]{3,1,0,2:T(8,128)}, ...), condition=%wide.region_24.25_spmd, body=%wide.region_21.24_spmd.sunk | while | flops 2498562 | bytes 7209049 | solution.py:57
  480.6 77.4 %while.184 = (s32[]{:T(128)}, f32[5,8192]{1,0:T(8,128)}, f32[5,8192]{1,0:T(8,128)}, f32[5,5,8192]{2,1,0:T(8,128)S(1)}, f32[5,8192]{1,0:T(8,128)S(1)}, /*index=5*/s32[]{:T(128)}) while((s32[]{:T(128)}, f32[5,8192]{1,0:T(8,128)}, f32[5,8192]{1,0:T(8,128)}, f32[5,5,8192]{2,1,0:T(8,128)S(1)}, f32[5,8192]{1,0:T(8,128)S(1)}, ...), condition=%wide.region_27.28_spmd, body=%wide.region_25.27_spmd.sunk | while | flops 409602 | bytes 2949257 | solution.py:173
  488.3 5.2 collective-permute-start.2
  498.3 5.2 collective-permute-start.2
  508.2 5.2 collective-permute-start.2
  518.2 5.2 collective-permute-start.2
  528.1 5.2 collective-permute-start.2
  538.1 5.2 collective-permute-start.2
  548.1 5.2 collective-permute-start.2
  559.0 54.0 %while.185 = (s32[]{:T(128)}, f32[5,8192]{1,0:T(8,128)S(1)}, f32[5,8,8192]{2,1,0:T(8,128)S(1)}, f32[5,5,8,8192]{3,2,1,0:T(8,128)}, f32[5,8,8192]{2,0,1:T(8,128)}...) while((s32[]{:T(128)}, f32[5,8192]{1,0:T(8,128)S(1)}, f32[5,8,8192]{2,1,0:T(8,128)S(1)}, ...), condition=%wide.region_30.31_spmd, body=%wide.region_28.30_spmd.sunk | while | flops 450562 | bytes 4096097 | solution.py:88
  560.0 3.6 constant_dynamic-slice_fusion.18
  566.8 3.6 constant_dynamic-slice_fusion.18
  614.2 42.2 %while.189 = (s32[]{:T(128)}, f32[5,5,8192]{2,1,0:T(8,128)S(1)}, f32[5,8192]{1,0:T(8,128)S(1)}, f32[5,5,8,8192]{3,1,0,2:T(8,128)}, f32[5,8,8192]{2,0,1:T(8,128)}...) while((s32[]{:T(128)}, f32[5,5,8192]{2,1,0:T(8,128)S(1)}, ...), condition=%wide.region_34.35_spmd.clone, body=%wide.region_31.34_spmd.clone.sunk | while | flops 2539527 | bytes 7700649 | solution.py:74
  657.8 80.3 %while.186 = (s32[]{:T(128)}, f32[5,8192]{1,0:T(8,128)}, f32[5,8192]{1,0:T(8,128)}, f32[5,5,8192]{2,1,0:T(8,128)S(1)}, f32[5,8192]{1,0:T(8,128)S(1)}, /*index=5*/s32[]{:T(128)}) while((s32[]{:T(128)}, f32[5,8192]{1,0:T(8,128)}, f32[5,8192]{1,0:T(8,128)}, f32[5,5,8192]{2,1,0:T(8,128)S(1)}, f32[5,8192]{1,0:T(8,128)S(1)}, ...), condition=%wide.region_37.38_spmd, body=%wide.region_35.37_spmd.sunk | while | flops 409602 | bytes 2949257 | solution.py:182
  659.7 7.5 collective-permute-done.3
  670.3 6.9 collective-permute-done.3
  680.3 6.9 collective-permute-done.3
  690.2 6.9 collective-permute-done.3
  700.2 6.9 collective-permute-done.3
  710.1 6.9 collective-permute-done.3
  720.1 6.9 collective-permute-done.3
  730.0 6.9 collective-permute-done.3
  739.0 65.9 %while.187 = (s32[]{:T(128)}, f32[5,8192]{1,0:T(8,128)S(1)}, f32[5,8,8192]{2,1,0:T(8,128)S(1)}, f32[5,8,8192]{2,1,0:T(8,128)}, f32[5,5,8,8192]{3,2,1,0:T(8,128)}...) while((s32[]{:T(128)}, f32[5,8192]{1,0:T(8,128)S(1)}, ...), condition=%wide.region_40.41_spmd, body=%wide.region_38.40_spmd.sunk | while | flops 491526 | bytes 4751523 | solution.py:102
  (579 shorter events, 519.0 us)
Async XLA Ops:
  0.6 1.5 copy-start.23
  0.6 1.7 copy-start.21
  3.0 1.2 copy-start.20
  3.0 8.9 %copy-start.11 = (f32[5,8,8192]{2,1,0:T(8,128)S(1)}, f32[5,8,8192]{2,1,0:T(8,128)}, u32[]{:S(2)}) copy-start(f32[5,8,8192]{2,1,0:T(8,128)} %param.36) | copy-start | bytes 3932164
  4.2 11.0 %copy-start.19 = (s32[8,8192]{1,0:T(8,128)S(1)}, s32[8,8192]{1,0:T(8,128)}, u32[]{:S(2)}) copy-start(s32[8,8192]{1,0:T(8,128)} %param.42) | copy-start | bytes 786436
  5.4 25.0 %all-to-all-start = ((f32[5,64,128]{2,0,1:T(8,128)}), f32[5,64,128]{2,0,1:T(8,128)}, u32[]{:S(2)}, u32[]{:S(2)}) async-start(f32[5,64,128]{2,0,1:T(8,128)} %copy.64), calls=%async_computation | async-start | bytes 524288 | tf_op jit(solution)/shard_map/all_to_all | solution.py:159
  11.9 26.4 %collective-permute-start.4 = (f32[5,8,1]{2,1,0:T(8,128)S(1)}, f32[5,8,1]{2,1,0:T(8,128)S(1)}, u32[]{:S(2)}, u32[]{:S(2)}) collective-permute-start(f32[5,8,1]{2,1,0:T(8,128)S(1)} %get-tuple-element.1570), channel_id=1, source_target_pairs={{0,1},{1,2},{2,3},{3,0},{4,5},{5,6},{6,7},{7,4},{8,9},{9,10},{10,1... | collective-permute-start | bytes 488 | tf_op jit(solution)/shard_map/ppermute | solution.py:17
  13.1 25.3 %collective-permute-start.5 = (f32[5,8,1]{2,1,0:T(8,128)S(1)}, f32[5,8,1]{2,1,0:T(8,128)S(1)}, u32[]{:S(2)}, u32[]{:S(2)}) collective-permute-start(f32[5,8,1]{2,1,0:T(8,128)S(1)} %get-tuple-element.1571), channel_id=1, source_target_pairs={{1,0},{2,1},{3,2},{0,3},{5,4},{6,5},{7,6},{4,7},{9,8},{10,9},{11,1... | collective-permute-start | bytes 488 | tf_op jit(solution)/shard_map/ppermute | solution.py:19
  15.9 11.0 %copy-start.16 = (f32[5,8,8192]{2,1,0:T(8,128)S(1)}, f32[5,8,8192]{2,1,0:T(8,128)}, u32[]{:S(2)}) copy-start(f32[5,8,8192]{2,1,0:T(8,128)} %param.39) | copy-start | bytes 3932164
  26.9 1.3 copy-start.17
  28.2 2.1 copy-start.22
  80.2 2.6 copy-start.4
  82.8 8.1 %copy-start.5 = (f32[5,8192]{1,0:T(8,128)S(1)}, f32[5,8192]{1,0:T(8,128)}, u32[]{:S(2)}) copy-start(f32[5,8192]{1,0:T(8,128)} %get-tuple-element.2061) | copy-start | bytes 491524 | tf_op jit(solution)/shard_map/while
  82.8 7.6 collective-permute-start
  90.5 1.2 copy-start
  91.6 9.4 %copy-start.5 = (f32[5,8192]{1,0:T(8,128)S(1)}, f32[5,8192]{1,0:T(8,128)}, u32[]{:S(2)}) copy-start(f32[5,8192]{1,0:T(8,128)} %get-tuple-element.2061) | copy-start | bytes 491524 | tf_op jit(solution)/shard_map/while
  91.6 8.9 %collective-permute-start = (f32[5,8192]{1,0:T(8,128)}, f32[5,8192]{1,0:T(8,128)S(1)}, u32[]{:S(2)}, u32[]{:S(2)}) collective-permute-start(f32[5,8192]{1,0:T(8,128)} %get-tuple-element.2052), channel_id=1, source_target_pairs={{0,4},{4,8},{8,12},{12,16},{16,20},{20,24},{24,28},{1,5},{5,9},{9,... | collective-permute-start | bytes 491528 | tf_op jit(solution)/shard_map/while/body/eval_jaxpr/ppermute | solution.py:29
  100.6 1.2 copy-start
  101.7 9.4 %copy-start.5 = (f32[5,8192]{1,0:T(8,128)S(1)}, f32[5,8192]{1,0:T(8,128)}, u32[]{:S(2)}) copy-start(f32[5,8192]{1,0:T(8,128)} %get-tuple-element.2061) | copy-start | bytes 491524 | tf_op jit(solution)/shard_map/while
  101.7 8.9 %collective-permute-start = (f32[5,8192]{1,0:T(8,128)}, f32[5,8192]{1,0:T(8,128)S(1)}, u32[]{:S(2)}, u32[]{:S(2)}) collective-permute-start(f32[5,8192]{1,0:T(8,128)} %get-tuple-element.2052), channel_id=1, source_target_pairs={{0,4},{4,8},{8,12},{12,16},{16,20},{20,24},{24,28},{1,5},{5,9},{9,... | collective-permute-start | bytes 491528 | tf_op jit(solution)/shard_map/while/body/eval_jaxpr/ppermute | solution.py:29
  110.7 1.2 copy-start
  111.8 9.4 %copy-start.5 = (f32[5,8192]{1,0:T(8,128)S(1)}, f32[5,8192]{1,0:T(8,128)}, u32[]{:S(2)}) copy-start(f32[5,8192]{1,0:T(8,128)} %get-tuple-element.2061) | copy-start | bytes 491524 | tf_op jit(solution)/shard_map/while
  111.8 8.9 %collective-permute-start = (f32[5,8192]{1,0:T(8,128)}, f32[5,8192]{1,0:T(8,128)S(1)}, u32[]{:S(2)}, u32[]{:S(2)}) collective-permute-start(f32[5,8192]{1,0:T(8,128)} %get-tuple-element.2052), channel_id=1, source_target_pairs={{0,4},{4,8},{8,12},{12,16},{16,20},{20,24},{24,28},{1,5},{5,9},{9,... | collective-permute-start | bytes 491528 | tf_op jit(solution)/shard_map/while/body/eval_jaxpr/ppermute | solution.py:29
  120.8 1.2 copy-start
  121.9 9.4 %copy-start.5 = (f32[5,8192]{1,0:T(8,128)S(1)}, f32[5,8192]{1,0:T(8,128)}, u32[]{:S(2)}) copy-start(f32[5,8192]{1,0:T(8,128)} %get-tuple-element.2061) | copy-start | bytes 491524 | tf_op jit(solution)/shard_map/while
  121.9 8.9 %collective-permute-start = (f32[5,8192]{1,0:T(8,128)}, f32[5,8192]{1,0:T(8,128)S(1)}, u32[]{:S(2)}, u32[]{:S(2)}) collective-permute-start(f32[5,8192]{1,0:T(8,128)} %get-tuple-element.2052), channel_id=1, source_target_pairs={{0,4},{4,8},{8,12},{12,16},{16,20},{20,24},{24,28},{1,5},{5,9},{9,... | collective-permute-start | bytes 491528 | tf_op jit(solution)/shard_map/while/body/eval_jaxpr/ppermute | solution.py:29
  130.9 1.2 copy-start
  132.0 9.4 %copy-start.5 = (f32[5,8192]{1,0:T(8,128)S(1)}, f32[5,8192]{1,0:T(8,128)}, u32[]{:S(2)}) copy-start(f32[5,8192]{1,0:T(8,128)} %get-tuple-element.2061) | copy-start | bytes 491524 | tf_op jit(solution)/shard_map/while
  132.0 8.9 %collective-permute-start = (f32[5,8192]{1,0:T(8,128)}, f32[5,8192]{1,0:T(8,128)S(1)}, u32[]{:S(2)}, u32[]{:S(2)}) collective-permute-start(f32[5,8192]{1,0:T(8,128)} %get-tuple-element.2052), channel_id=1, source_target_pairs={{0,4},{4,8},{8,12},{12,16},{16,20},{20,24},{24,28},{1,5},{5,9},{9,... | collective-permute-start | bytes 491528 | tf_op jit(solution)/shard_map/while/body/eval_jaxpr/ppermute | solution.py:29
  142.1 9.4 %copy-start.5 = (f32[5,8192]{1,0:T(8,128)S(1)}, f32[5,8192]{1,0:T(8,128)}, u32[]{:S(2)}) copy-start(f32[5,8192]{1,0:T(8,128)} %get-tuple-element.2061) | copy-start | bytes 491524 | tf_op jit(solution)/shard_map/while
  142.1 8.9 %collective-permute-start = (f32[5,8192]{1,0:T(8,128)}, f32[5,8192]{1,0:T(8,128)S(1)}, u32[]{:S(2)}, u32[]{:S(2)}) collective-permute-start(f32[5,8192]{1,0:T(8,128)} %get-tuple-element.2052), channel_id=1, source_target_pairs={{0,4},{4,8},{8,12},{12,16},{16,20},{20,24},{24,28},{1,5},{5,9},{9,... | collective-permute-start | bytes 491528 | tf_op jit(solution)/shard_map/while/body/eval_jaxpr/ppermute | solution.py:29
  152.2 9.4 %copy-start.5 = (f32[5,8192]{1,0:T(8,128)S(1)}, f32[5,8192]{1,0:T(8,128)}, u32[]{:S(2)}) copy-start(f32[5,8192]{1,0:T(8,128)} %get-tuple-element.2061) | copy-start | bytes 491524 | tf_op jit(solution)/shard_map/while
  152.2 8.9 %collective-permute-start = (f32[5,8192]{1,0:T(8,128)}, f32[5,8192]{1,0:T(8,128)S(1)}, u32[]{:S(2)}, u32[]{:S(2)}) collective-permute-start(f32[5,8192]{1,0:T(8,128)} %get-tuple-element.2052), channel_id=1, source_target_pairs={{0,4},{4,8},{8,12},{12,16},{16,20},{20,24},{24,28},{1,5},{5,9},{9,... | collective-permute-start | bytes 491528 | tf_op jit(solution)/shard_map/while/body/eval_jaxpr/ppermute | solution.py:29
  251.5 9.4 %collective-permute-start.1 = (f32[5,8192]{1,0:T(8,128)}, f32[5,8192]{1,0:T(8,128)S(1)}, u32[]{:S(2)}, u32[]{:S(2)}) collective-permute-start(f32[5,8192]{1,0:T(8,128)} %get-tuple-element.2124), channel_id=1, source_target_pairs={{4,0},{8,4},{12,8},{16,12},{20,16},{24,20},{28,24},{5,1},{9,5},{13... | collective-permute-start | bytes 491528 | tf_op jit(solution)/shard_map/while/body/eval_jaxpr/ppermute | solution.py:29
  262.1 8.8 %collective-permute-start.1 = (f32[5,8192]{1,0:T(8,128)}, f32[5,8192]{1,0:T(8,128)S(1)}, u32[]{:S(2)}, u32[]{:S(2)}) collective-permute-start(f32[5,8192]{1,0:T(8,128)} %get-tuple-element.2124), channel_id=1, source_target_pairs={{4,0},{8,4},{12,8},{16,12},{20,16},{24,20},{28,24},{5,1},{9,5},{13... | collective-permute-start | bytes 491528 | tf_op jit(solution)/shard_map/while/body/eval_jaxpr/ppermute | solution.py:29
  272.1 8.8 %collective-permute-start.1 = (f32[5,8192]{1,0:T(8,128)}, f32[5,8192]{1,0:T(8,128)S(1)}, u32[]{:S(2)}, u32[]{:S(2)}) collective-permute-start(f32[5,8192]{1,0:T(8,128)} %get-tuple-element.2124), channel_id=1, source_target_pairs={{4,0},{8,4},{12,8},{16,12},{20,16},{24,20},{28,24},{5,1},{9,5},{13... | collective-permute-start | bytes 491528 | tf_op jit(solution)/shard_map/while/body/eval_jaxpr/ppermute | solution.py:29
  282.1 8.8 %collective-permute-start.1 = (f32[5,8192]{1,0:T(8,128)}, f32[5,8192]{1,0:T(8,128)S(1)}, u32[]{:S(2)}, u32[]{:S(2)}) collective-permute-start(f32[5,8192]{1,0:T(8,128)} %get-tuple-element.2124), channel_id=1, source_target_pairs={{4,0},{8,4},{12,8},{16,12},{20,16},{24,20},{28,24},{5,1},{9,5},{13... | collective-permute-start | bytes 491528 | tf_op jit(solution)/shard_map/while/body/eval_jaxpr/ppermute | solution.py:29
  292.0 8.8 %collective-permute-start.1 = (f32[5,8192]{1,0:T(8,128)}, f32[5,8192]{1,0:T(8,128)S(1)}, u32[]{:S(2)}, u32[]{:S(2)}) collective-permute-start(f32[5,8192]{1,0:T(8,128)} %get-tuple-element.2124), channel_id=1, source_target_pairs={{4,0},{8,4},{12,8},{16,12},{20,16},{24,20},{28,24},{5,1},{9,5},{13... | collective-permute-start | bytes 491528 | tf_op jit(solution)/shard_map/while/body/eval_jaxpr/ppermute | solution.py:29
  302.0 8.8 %collective-permute-start.1 = (f32[5,8192]{1,0:T(8,128)}, f32[5,8192]{1,0:T(8,128)S(1)}, u32[]{:S(2)}, u32[]{:S(2)}) collective-permute-start(f32[5,8192]{1,0:T(8,128)} %get-tuple-element.2124), channel_id=1, source_target_pairs={{4,0},{8,4},{12,8},{16,12},{20,16},{24,20},{28,24},{5,1},{9,5},{13... | collective-permute-start | bytes 491528 | tf_op jit(solution)/shard_map/while/body/eval_jaxpr/ppermute | solution.py:29
  311.9 8.8 %collective-permute-start.1 = (f32[5,8192]{1,0:T(8,128)}, f32[5,8192]{1,0:T(8,128)S(1)}, u32[]{:S(2)}, u32[]{:S(2)}) collective-permute-start(f32[5,8192]{1,0:T(8,128)} %get-tuple-element.2124), channel_id=1, source_target_pairs={{4,0},{8,4},{12,8},{16,12},{20,16},{24,20},{28,24},{5,1},{9,5},{13... | collective-permute-start | bytes 491528 | tf_op jit(solution)/shard_map/while/body/eval_jaxpr/ppermute | solution.py:29
  321.9 8.8 %collective-permute-start.1 = (f32[5,8192]{1,0:T(8,128)}, f32[5,8192]{1,0:T(8,128)S(1)}, u32[]{:S(2)}, u32[]{:S(2)}) collective-permute-start(f32[5,8192]{1,0:T(8,128)} %get-tuple-element.2124), channel_id=1, source_target_pairs={{4,0},{8,4},{12,8},{16,12},{20,16},{24,20},{28,24},{5,1},{9,5},{13... | collective-permute-start | bytes 491528 | tf_op jit(solution)/shard_map/while/body/eval_jaxpr/ppermute | solution.py:29
  333.0 82.2 %copy-start.12 = (f32[5,8,8192]{2,1,0:T(8,128)S(1)}, f32[5,8,8192]{2,1,0:T(8,128)}, u32[]{:S(2)}) copy-start(f32[5,8,8192]{2,1,0:T(8,128)} %param.36) | copy-start | bytes 3932164
  419.8 13.1 %all-to-all-start.1 = ((f32[5,64,128]{2,0,1:T(8,128)}), f32[5,64,128]{2,0,1:T(8,128)S(1)}, u32[]{:S(2)}, u32[]{:S(2)}) async-start(f32[5,64,128]{2,0,1:T(8,128)} %copy.77), calls=%async_computation.1 | async-start | bytes 524288 | tf_op jit(solution)/shard_map/all_to_all | solution.py:159
  422.7 13.9 %collective-permute-start.6 = (f32[5,8,1]{2,1,0:T(8,128)S(1)}, f32[5,8,1]{2,1,0:T(8,128)S(1)}, u32[]{:S(2)}, u32[]{:S(2)}) collective-permute-start(f32[5,8,1]{2,1,0:T(8,128)S(1)} %get-tuple-element.1568), channel_id=1, source_target_pairs={{0,1},{1,2},{2,3},{3,0},{4,5},{5,6},{6,7},{7,4},{8,9},{9,10},{10,1... | collective-permute-start | bytes 488 | tf_op jit(solution)/shard_map/ppermute | solution.py:17
  423.9 12.8 %collective-permute-start.7 = (f32[5,8,1]{2,1,0:T(8,128)S(1)}, f32[5,8,1]{2,1,0:T(8,128)S(1)}, u32[]{:S(2)}, u32[]{:S(2)}) collective-permute-start(f32[5,8,1]{2,1,0:T(8,128)S(1)} %get-tuple-element.1569), channel_id=1, source_target_pairs={{1,0},{2,1},{3,2},{0,3},{5,4},{6,5},{7,6},{4,7},{9,8},{10,9},{11,1... | collective-permute-start | bytes 488 | tf_op jit(solution)/shard_map/ppermute | solution.py:19
  435.1 1.6 copy-start.15
  435.1 1.6 copy-start.18
  480.6 6.6 collective-permute-start.2
  488.3 8.8 %collective-permute-start.2 = (f32[5,8192]{1,0:T(8,128)}, f32[5,8192]{1,0:T(8,128)S(1)}, u32[]{:S(2)}, u32[]{:S(2)}) collective-permute-start(f32[5,8192]{1,0:T(8,128)} %get-tuple-element.2193), channel_id=1, source_target_pairs={{0,4},{4,8},{8,12},{12,16},{16,20},{20,24},{24,28},{1,5},{5,9},{9,... | collective-permute-start | bytes 491528 | tf_op jit(solution)/shard_map/while/body/eval_jaxpr/ppermute | solution.py:29
  498.3 8.8 %collective-permute-start.2 = (f32[5,8192]{1,0:T(8,128)}, f32[5,8192]{1,0:T(8,128)S(1)}, u32[]{:S(2)}, u32[]{:S(2)}) collective-permute-start(f32[5,8192]{1,0:T(8,128)} %get-tuple-element.2193), channel_id=1, source_target_pairs={{0,4},{4,8},{8,12},{12,16},{16,20},{20,24},{24,28},{1,5},{5,9},{9,... | collective-permute-start | bytes 491528 | tf_op jit(solution)/shard_map/while/body/eval_jaxpr/ppermute | solution.py:29
  508.2 8.8 %collective-permute-start.2 = (f32[5,8192]{1,0:T(8,128)}, f32[5,8192]{1,0:T(8,128)S(1)}, u32[]{:S(2)}, u32[]{:S(2)}) collective-permute-start(f32[5,8192]{1,0:T(8,128)} %get-tuple-element.2193), channel_id=1, source_target_pairs={{0,4},{4,8},{8,12},{12,16},{16,20},{20,24},{24,28},{1,5},{5,9},{9,... | collective-permute-start | bytes 491528 | tf_op jit(solution)/shard_map/while/body/eval_jaxpr/ppermute | solution.py:29
  518.2 8.8 %collective-permute-start.2 = (f32[5,8192]{1,0:T(8,128)}, f32[5,8192]{1,0:T(8,128)S(1)}, u32[]{:S(2)}, u32[]{:S(2)}) collective-permute-start(f32[5,8192]{1,0:T(8,128)} %get-tuple-element.2193), channel_id=1, source_target_pairs={{0,4},{4,8},{8,12},{12,16},{16,20},{20,24},{24,28},{1,5},{5,9},{9,... | collective-permute-start | bytes 491528 | tf_op jit(solution)/shard_map/while/body/eval_jaxpr/ppermute | solution.py:29
  528.1 8.8 %collective-permute-start.2 = (f32[5,8192]{1,0:T(8,128)}, f32[5,8192]{1,0:T(8,128)S(1)}, u32[]{:S(2)}, u32[]{:S(2)}) collective-permute-start(f32[5,8192]{1,0:T(8,128)} %get-tuple-element.2193), channel_id=1, source_target_pairs={{0,4},{4,8},{8,12},{12,16},{16,20},{20,24},{24,28},{1,5},{5,9},{9,... | collective-permute-start | bytes 491528 | tf_op jit(solution)/shard_map/while/body/eval_jaxpr/ppermute | solution.py:29
  538.1 8.8 %collective-permute-start.2 = (f32[5,8192]{1,0:T(8,128)}, f32[5,8192]{1,0:T(8,128)S(1)}, u32[]{:S(2)}, u32[]{:S(2)}) collective-permute-start(f32[5,8192]{1,0:T(8,128)} %get-tuple-element.2193), channel_id=1, source_target_pairs={{0,4},{4,8},{8,12},{12,16},{16,20},{20,24},{24,28},{1,5},{5,9},{9,... | collective-permute-start | bytes 491528 | tf_op jit(solution)/shard_map/while/body/eval_jaxpr/ppermute | solution.py:29
  548.1 8.8 %collective-permute-start.2 = (f32[5,8192]{1,0:T(8,128)}, f32[5,8192]{1,0:T(8,128)S(1)}, u32[]{:S(2)}, u32[]{:S(2)}) collective-permute-start(f32[5,8192]{1,0:T(8,128)} %get-tuple-element.2193), channel_id=1, source_target_pairs={{0,4},{4,8},{8,12},{12,16},{16,20},{20,24},{24,28},{1,5},{5,9},{9,... | collective-permute-start | bytes 491528 | tf_op jit(solution)/shard_map/while/body/eval_jaxpr/ppermute | solution.py:29
  657.8 9.4 %collective-permute-start.3 = (f32[5,8192]{1,0:T(8,128)}, f32[5,8192]{1,0:T(8,128)S(1)}, u32[]{:S(2)}, u32[]{:S(2)}) collective-permute-start(f32[5,8192]{1,0:T(8,128)} %get-tuple-element.2265), channel_id=1, source_target_pairs={{4,0},{8,4},{12,8},{16,12},{20,16},{24,20},{28,24},{5,1},{9,5},{13... | collective-permute-start | bytes 491528 | tf_op jit(solution)/shard_map/while/body/eval_jaxpr/ppermute | solution.py:29
  668.4 8.8 %collective-permute-start.3 = (f32[5,8192]{1,0:T(8,128)}, f32[5,8192]{1,0:T(8,128)S(1)}, u32[]{:S(2)}, u32[]{:S(2)}) collective-permute-start(f32[5,8192]{1,0:T(8,128)} %get-tuple-element.2265), channel_id=1, source_target_pairs={{4,0},{8,4},{12,8},{16,12},{20,16},{24,20},{28,24},{5,1},{9,5},{13... | collective-permute-start | bytes 491528 | tf_op jit(solution)/shard_map/while/body/eval_jaxpr/ppermute | solution.py:29
  678.3 8.8 %collective-permute-start.3 = (f32[5,8192]{1,0:T(8,128)}, f32[5,8192]{1,0:T(8,128)S(1)}, u32[]{:S(2)}, u32[]{:S(2)}) collective-permute-start(f32[5,8192]{1,0:T(8,128)} %get-tuple-element.2265), channel_id=1, source_target_pairs={{4,0},{8,4},{12,8},{16,12},{20,16},{24,20},{28,24},{5,1},{9,5},{13... | collective-permute-start | bytes 491528 | tf_op jit(solution)/shard_map/while/body/eval_jaxpr/ppermute | solution.py:29
  688.3 8.8 %collective-permute-start.3 = (f32[5,8192]{1,0:T(8,128)}, f32[5,8192]{1,0:T(8,128)S(1)}, u32[]{:S(2)}, u32[]{:S(2)}) collective-permute-start(f32[5,8192]{1,0:T(8,128)} %get-tuple-element.2265), channel_id=1, source_target_pairs={{4,0},{8,4},{12,8},{16,12},{20,16},{24,20},{28,24},{5,1},{9,5},{13... | collective-permute-start | bytes 491528 | tf_op jit(solution)/shard_map/while/body/eval_jaxpr/ppermute | solution.py:29
  698.3 8.8 %collective-permute-start.3 = (f32[5,8192]{1,0:T(8,128)}, f32[5,8192]{1,0:T(8,128)S(1)}, u32[]{:S(2)}, u32[]{:S(2)}) collective-permute-start(f32[5,8192]{1,0:T(8,128)} %get-tuple-element.2265), channel_id=1, source_target_pairs={{4,0},{8,4},{12,8},{16,12},{20,16},{24,20},{28,24},{5,1},{9,5},{13... | collective-permute-start | bytes 491528 | tf_op jit(solution)/shard_map/while/body/eval_jaxpr/ppermute | solution.py:29
  708.2 8.8 %collective-permute-start.3 = (f32[5,8192]{1,0:T(8,128)}, f32[5,8192]{1,0:T(8,128)S(1)}, u32[]{:S(2)}, u32[]{:S(2)}) collective-permute-start(f32[5,8192]{1,0:T(8,128)} %get-tuple-element.2265), channel_id=1, source_target_pairs={{4,0},{8,4},{12,8},{16,12},{20,16},{24,20},{28,24},{5,1},{9,5},{13... | collective-permute-start | bytes 491528 | tf_op jit(solution)/shard_map/while/body/eval_jaxpr/ppermute | solution.py:29
  718.2 8.8 %collective-permute-start.3 = (f32[5,8192]{1,0:T(8,128)}, f32[5,8192]{1,0:T(8,128)S(1)}, u32[]{:S(2)}, u32[]{:S(2)}) collective-permute-start(f32[5,8192]{1,0:T(8,128)} %get-tuple-element.2265), channel_id=1, source_target_pairs={{4,0},{8,4},{12,8},{16,12},{20,16},{24,20},{28,24},{5,1},{9,5},{13... | collective-permute-start | bytes 491528 | tf_op jit(solution)/shard_map/while/body/eval_jaxpr/ppermute | solution.py:29
  728.1 8.8 %collective-permute-start.3 = (f32[5,8192]{1,0:T(8,128)}, f32[5,8192]{1,0:T(8,128)S(1)}, u32[]{:S(2)}, u32[]{:S(2)}) collective-permute-start(f32[5,8192]{1,0:T(8,128)} %get-tuple-element.2265), channel_id=1, source_target_pairs={{4,0},{8,4},{12,8},{16,12},{20,16},{24,20},{28,24},{5,1},{9,5},{13... | collective-permute-start | bytes 491528 | tf_op jit(solution)/shard_map/while/body/eval_jaxpr/ppermute | solution.py:29
  804.9 1.5 copy-start.14
  (34 other events, 38.4 us)
where the time goes:
time: 813 us; the launch traced here: 806 us
  other arithmetic  254 us (31%)
  local copies, waits for them, and re-layouts  238 us (29%)
  waiting for transfers between devices  176 us (22%)
  starting transfers between devices  127 us (16%)
    ppermute x32, waiting for transfers between devices, passed_along(): lax.ppermute(value, axis, [(source, source + steps) for source in range(i...  169 us
    dynamic_slice x48, local copies, waits for them, and re-layouts, plane_of(): return lax.dynamic_index_in_dim(array, index, axis, keepdims=False)  129 us
    reduce_sum x96, other arithmetic, apply_block(): return jnp.sum(block_inv * vector[None], axis=1)  116 us
    ppermute x32, starting transfers between devices, passed_along(): lax.ppermute(value, axis, [(source, source + steps) for source in range(i...  111 us
    dynamic_update_slice x32, local copies, waits for them, and re-layouts, step(): return (face, lax.dynamic_update_index_in_dim(sweep_output, face, index, 1))  54.3 us
    unnamed x46, local copies, waits for them, and re-layouts  22.3 us
    reduce_sum x32, other arithmetic, multiply_maps(): return jnp.sum(left[:, :, None, :] * right[None], axis=1)  21.3 us
    add x16, other arithmetic, step(): plane_of(driving_term, index, 1) + plane_of(decay, index, 1) * face  17.3 us
  transfers between devices with their start and end apart: 38, of which 33 were waited for; matrix products, arithmetic and copies ran while one was open for 3% of the time, Pallas kernels for 0%

commit v1 on v0

--- a/solution.py
+++ b/solution.py
@@ -5,6 +5,19 @@
 
 ITERS = 2
 CAP = 2
+
+
+def _draft_spans(out_dim, sheet, which_dim):
+    work_now = jnp.concatenate(
+        lax.all_to_all(
+            jnp.stack(jnp.split(sheet, lax.axis_size(("stream", "cross")), axis=which_dim), 0),
+            ("stream", "cross"),
+            0,
+            0,
+        ),
+        out_dim,
+    )
+    return work_now
 
 
 def padded_2(cells, sides, width):
@@ -156,9 +169,7 @@
         )
         values = stencil_weight[None] * (selected_values + displaced_values)
         outgoing = jnp.einsum("se,vep->vsp", place_table, values, precision=lax.Precision.HIGHEST)
-        received = lax.all_to_all(
-            outgoing, ("stream", "cross"), split_axis=1, concat_axis=1, tiled=True
-        )
+        received = _draft_spans(1, outgoing, 1)
         fringe = jnp.einsum(
             "bs,vsp->vbp", onehot, received, precision=lax.Precision.HIGHEST
         ).reshape(state.shape)

time: 813 us -> 848 us (1.043)
  local copies, waits for them, and re-layouts: 238 us -> 276 us
    unnamed x46 -> x108, local copies, waits for them, and re-layouts: 22.3 us -> 59.3 us
where the time goes in v1:
time: 848 us; the launch traced here: 842 us
  local copies, waits for them, and re-layouts  276 us (33%)
  other arithmetic  254 us (30%)
  waiting for transfers between devices  174 us (21%)
  starting transfers between devices  127 us (15%)
    ppermute x32, waiting for transfers between devices, passed_along(): lax.ppermute(value, axis, [(source, source + steps) for source in range(i...  169 us
    dynamic_slice x48, local copies, waits for them, and re-layouts, plane_of(): return lax.dynamic_index_in_dim(array, index, axis, keepdims=False)  129 us
    reduce_sum x96, other arithmetic, apply_block(): return jnp.sum(block_inv * vector[None], axis=1)  116 us
    ppermute x32, starting transfers between devices, passed_along(): lax.ppermute(value, axis, [(source, source + steps) for source in range(i...  111 us
    unnamed x108, local copies, waits for them, and re-layouts  59.3 us
    dynamic_update_slice x32, local copies, waits for them, and re-layouts, step(): return (face, lax.dynamic_update_index_in_dim(sweep_output, face, index, 1))  54.3 us
    reduce_sum x32, other arithmetic, multiply_maps(): return jnp.sum(left[:, :, None, :] * right[None], axis=1)  21.3 us
    add x16, other arithmetic, step(): plane_of(driving_term, index, 1) + plane_of(decay, index, 1) * face  17.3 us
  transfers between devices with their start and end apart: 38, of which 33 were waited for; matrix products, arithmetic and copies ran while one was open for 3% of the time, Pallas kernels for 0%

profile of v1, /device:TPU:3, one launch (start us, length us, event | category | flops | bytes accessed | tf_op | source)
XLA Modules:
  0.0 841.6 jit_solution(70006610215615546)
XLA Ops:
  23.7 6.5 all-to-all-start
  34.3 11.0 %copy.51 = f32[5,5,8,8192]{3,1,0,2:T(8,128)} copy(f32[5,5,8,8192]{3,2,1,0:T(8,128)} %param.38) | data formatting | bytes 13107200
  62.3 36.2 %while.178 = (s32[]{:T(128)}, f32[5,5,8192]{2,1,0:T(8,128)S(1)}, f32[5,8192]{1,0:T(8,128)}, f32[5,5,8,8192]{3,1,0,2:T(8,128)}, f32[5,8,8192]{2,0,1:T(8,128)S(1)}, /*index=5*/f32[5,8,8192]{2,0,1:T(8,128)}, s32[]{:T(128)}) while((s32[]{:T(128)}, f32[5,5,8192]{2,1,0:T(8,128)S(1)}, f32[5,8192]{1,0:T(8,128)}, f32[5,5,8,8192]{3,1,0,2:T(8,128)}, ...), condition=%wide.region_4.5_spmd, body=%wide.region_1.4_spmd.sunk | while | flops 2498562 | bytes 7209049 | solution.py:70
  101.2 79.5 %while.179 = (s32[]{:T(128)}, f32[5,8192]{1,0:T(8,128)}, f32[5,8192]{1,0:T(8,128)}, f32[5,5,8192]{2,1,0:T(8,128)S(1)}, f32[5,8192]{1,0:T(8,128)}, /*index=5*/s32[]{:T(128)}) while((s32[]{:T(128)}, f32[5,8192]{1,0:T(8,128)}, f32[5,8192]{1,0:T(8,128)}, f32[5,5,8192]{2,1,0:T(8,128)S(1)}, f32[5,8192]{1,0:T(8,128)}, /*index=5*/s32[]{:T(128)}) %tuple.342), condition=%wide.region_7.8_spmd, body=%wide.region_5.7_spmd.sunk | while | flops 409602 | bytes 3604645 | solution.py:184
  101.2 4.0 collective-permute-start
  110.0 5.3 collective-permute-start
  120.1 5.3 collective-permute-start
  130.2 5.3 collective-permute-start
  140.3 5.3 collective-permute-start
  150.4 5.3 collective-permute-start
  160.5 5.3 collective-permute-start
  170.6 5.3 collective-permute-start
  181.6 54.0 %while.180 = (s32[]{:T(128)}, f32[5,8192]{1,0:T(8,128)S(1)}, f32[5,8,8192]{2,1,0:T(8,128)S(1)}, f32[5,5,8,8192]{3,2,1,0:T(8,128)}, f32[5,8,8192]{2,0,1:T(8,128)}...) while((s32[]{:T(128)}, f32[5,8192]{1,0:T(8,128)S(1)}, f32[5,8,8192]{2,1,0:T(8,128)S(1)}, ...), condition=%wide.region_10.11_spmd, body=%wide.region_8.10_spmd.sunk | while | flops 450562 | bytes 4096097 | solution.py:101
  182.7 3.6 constant_dynamic-slice_fusion.16
  189.5 3.6 constant_dynamic-slice_fusion.16
  196.2 3.6 constant_dynamic-slice_fusion.16
  203.0 3.6 constant_dynamic-slice_fusion.16
  209.7 3.6 constant_dynamic-slice_fusion.16
  216.5 3.6 constant_dynamic-slice_fusion.16
  223.2 3.6 constant_dynamic-slice_fusion.16
  230.0 3.6 constant_dynamic-slice_fusion.16
  236.6 31.9 %while.188 = (s32[]{:T(128)}, f32[5,5,8192]{2,1,0:T(8,128)S(1)}, f32[5,8192]{1,0:T(8,128)S(1)}, f32[5,5,8,8192]{3,1,0,2:T(8,128)}, f32[5,8,8192]{2,0,1:T(8,128)}...) while((s32[]{:T(128)}, f32[5,5,8192]{2,1,0:T(8,128)S(1)}, ...), condition=%wide.region_14.15_spmd.clone, body=%wide.region_11.14_spmd.clone.sunk | while | flops 2539527 | bytes 7700649 | solution.py:87
  269.9 80.3 %while.181 = (s32[]{:T(128)}, f32[5,8192]{1,0:T(8,128)}, f32[5,8192]{1,0:T(8,128)}, f32[5,5,8192]{2,1,0:T(8,128)S(1)}, f32[5,8192]{1,0:T(8,128)S(1)}, /*index=5*/s32[]{:T(128)}) while((s32[]{:T(128)}, f32[5,8192]{1,0:T(8,128)}, f32[5,8192]{1,0:T(8,128)}, f32[5,5,8192]{2,1,0:T(8,128)S(1)}, f32[5,8192]{1,0:T(8,128)S(1)}, ...), condition=%wide.region_17.18_spmd, body=%wide.region_15.17_spmd.sunk | while | flops 409602 | bytes 2949257 | solution.py:193
  271.8 7.5 collective-permute-done.1
  282.4 6.9 collective-permute-done.1
  292.4 6.9 collective-permute-done.1
  302.3 6.9 collective-permute-done.1
  312.3 6.9 collective-permute-done.1
  322.2 6.9 collective-permute-done.1
  332.2 6.9 collective-permute-done.1
  342.1 6.9 collective-permute-done.1
  351.3 82.2 %while.182 = (s32[]{:T(128)}, f32[5,8192]{1,0:T(8,128)S(1)}, f32[5,8,8192]{2,1,0:T(8,128)}, f32[5,8,8192]{2,1,0:T(8,128)S(1)}, f32[5,5,8,8192]{3,2,1,0:T(8,128)}...) while((s32[]{:T(128)}, f32[5,8192]{1,0:T(8,128)S(1)}, ...), condition=%wide.region_20.21_spmd, body=%wide.region_18.20_spmd.sunk | while | flops 491526 | bytes 4751523 | solution.py:115
  351.3 3.7 constant_dynamic-slice_fusion.17
  357.4 4.2 dynamic_update_slice.41
  367.6 4.2 dynamic_update_slice.41
  377.9 4.2 dynamic_update_slice.41
  388.1 4.2 dynamic_update_slice.41
  398.4 4.2 dynamic_update_slice.41
  408.7 4.2 dynamic_update_slice.41
  418.9 4.2 dynamic_update_slice.41
  429.2 4.2 dynamic_update_slice.41
  462.7 4.8 all-to-all-done.1
  475.7 38.1 %while.183 = (s32[]{:T(128)}, f32[5,5,8192]{2,1,0:T(8,128)S(1)}, f32[5,8192]{1,0:T(8,128)S(1)}, f32[5,5,8,8192]{3,1,0,2:T(8,128)}, f32[5,8,8192]{2,0,1:T(8,128)}, /*index=5*/f32[5,8,8192]{2,0,1:T(8,128)}, s32[]{:T(128)}) while((s32[]{:T(128)}, f32[5,5,8192]{2,1,0:T(8,128)S(1)}, f32[5,8192]{1,0:T(8,128)S(1)}, f32[5,5,8,8192]{3,1,0,2:T(8,128)}, ...), condition=%wide.region_24.25_spmd, body=%wide.region_21.24_spmd.sunk | while | flops 2498562 | bytes 7209049 | solution.py:70
  515.2 78.0 %while.184 = (s32[]{:T(128)}, f32[5,8192]{1,0:T(8,128)}, f32[5,8192]{1,0:T(8,128)}, f32[5,5,8192]{2,1,0:T(8,128)S(1)}, f32[5,8192]{1,0:T(8,128)S(1)}, /*index=5*/s32[]{:T(128)}) while((s32[]{:T(128)}, f32[5,8192]{1,0:T(8,128)}, f32[5,8192]{1,0:T(8,128)}, f32[5,5,8192]{2,1,0:T(8,128)S(1)}, f32[5,8192]{1,0:T(8,128)S(1)}, ...), condition=%wide.region_27.28_spmd, body=%wide.region_25.27_spmd.sunk | while | flops 409602 | bytes 2949257 | solution.py:184
  523.5 5.2 collective-permute-start.2
  533.5 5.2 collective-permute-start.2
  543.4 5.2 collective-permute-start.2
  553.4 5.2 collective-permute-start.2
  563.4 5.2 collective-permute-start.2
  573.3 5.2 collective-permute-start.2
  583.3 5.2 collective-permute-start.2
  594.2 54.0 %while.185 = (s32[]{:T(128)}, f32[5,8192]{1,0:T(8,128)S(1)}, f32[5,8,8192]{2,1,0:T(8,128)S(1)}, f32[5,5,8,8192]{3,2,1,0:T(8,128)}, f32[5,8,8192]{2,0,1:T(8,128)}...) while((s32[]{:T(128)}, f32[5,8192]{1,0:T(8,128)S(1)}, f32[5,8,8192]{2,1,0:T(8,128)S(1)}, ...), condition=%wide.region_30.31_spmd, body=%wide.region_28.30_spmd.sunk | while | flops 450562 | bytes 4096097 | solution.py:101
  595.3 3.6 constant_dynamic-slice_fusion.18
  649.4 42.2 %while.189 = (s32[]{:T(128)}, f32[5,5,8192]{2,1,0:T(8,128)S(1)}, f32[5,8192]{1,0:T(8,128)S(1)}, f32[5,5,8,8192]{3,1,0,2:T(8,128)}, f32[5,8,8192]{2,0,1:T(8,128)}...) while((s32[]{:T(128)}, f32[5,5,8192]{2,1,0:T(8,128)S(1)}, ...), condition=%wide.region_34.35_spmd.clone, body=%wide.region_31.34_spmd.clone.sunk | while | flops 2539527 | bytes 7700649 | solution.py:87
  693.0 80.3 %while.186 = (s32[]{:T(128)}, f32[5,8192]{1,0:T(8,128)}, f32[5,8192]{1,0:T(8,128)}, f32[5,5,8192]{2,1,0:T(8,128)S(1)}, f32[5,8192]{1,0:T(8,128)S(1)}, /*index=5*/s32[]{:T(128)}) while((s32[]{:T(128)}, f32[5,8192]{1,0:T(8,128)}, f32[5,8192]{1,0:T(8,128)}, f32[5,5,8192]{2,1,0:T(8,128)S(1)}, f32[5,8192]{1,0:T(8,128)S(1)}, ...), condition=%wide.region_37.38_spmd, body=%wide.region_35.37_spmd.sunk | while | flops 409602 | bytes 2949257 | solution.py:193
  694.9 7.5 collective-permute-done.3
  705.5 6.9 collective-permute-done.3
  715.5 6.9 collective-permute-done.3
  725.4 6.9 collective-permute-done.3
  735.4 6.9 collective-permute-done.3
  745.4 6.9 collective-permute-done.3
  755.3 6.9 collective-permute-done.3
  765.3 6.9 collective-permute-done.3
  774.3 65.9 %while.187 = (s32[]{:T(128)}, f32[5,8192]{1,0:T(8,128)S(1)}, f32[5,8,8192]{2,1,0:T(8,128)S(1)}, f32[5,8,8192]{2,1,0:T(8,128)}, f32[5,5,8,8192]{3,2,1,0:T(8,128)}...) while((s32[]{:T(128)}, f32[5,8192]{1,0:T(8,128)S(1)}, ...), condition=%wide.region_40.41_spmd, body=%wide.region_38.40_spmd.sunk | while | flops 491526 | bytes 4751523 | solution.py:115
  (643 shorter events, 556.3 us)
Async XLA Ops:
  0.6 1.5 copy-start.23
  0.6 1.7 copy-start.21
  3.0 1.2 copy-start.20
  3.0 27.2 %copy-start.11 = (f32[5,8,8192]{2,1,0:T(8,128)S(1)}, f32[5,8,8192]{2,1,0:T(8,128)}, u32[]{:S(2)}) copy-start(f32[5,8,8192]{2,1,0:T(8,128)} %param.36) | copy-start | bytes 3932164
  3.0 30.5 %copy-start.19 = (s32[8,8192]{1,0:T(8,128)S(1)}, s32[8,8192]{1,0:T(8,128)}, u32[]{:S(2)}) copy-start(s32[8,8192]{1,0:T(8,128)} %param.42) | copy-start | bytes 786436
  23.7 25.0 %all-to-all-start = ((f32[32,5,2,128]{3,2,1,0:T(2,128)}), f32[32,5,2,128]{3,2,1,0:T(2,128)}, u32[]{:S(2)}, u32[]{:S(2)}) async-start(f32[32,5,2,128]{3,2,1,0:T(2,128)} %constant_dynamic-update-slice_fusion), calls=%async_computation | async-start | bytes 327680 | tf_op jit(solution)/shard_map/all_to_all | solution.py:12
  30.3 26.5 %collective-permute-start.4 = (f32[5,8,1]{2,1,0:T(8,128)S(1)}, f32[5,8,1]{2,1,0:T(8,128)S(1)}, u32[]{:S(2)}, u32[]{:S(2)}) collective-permute-start(f32[5,8,1]{2,1,0:T(8,128)S(1)} %get-tuple-element.1522), channel_id=1, source_target_pairs={{0,1},{1,2},{2,3},{3,0},{4,5},{5,6},{6,7},{7,4},{8,9},{9,10},{10,1... | collective-permute-start | bytes 488 | tf_op jit(solution)/shard_map/ppermute | solution.py:30
  31.5 25.3 %collective-permute-start.5 = (f32[5,8,1]{2,1,0:T(8,128)S(1)}, f32[5,8,1]{2,1,0:T(8,128)S(1)}, u32[]{:S(2)}, u32[]{:S(2)}) collective-permute-start(f32[5,8,1]{2,1,0:T(8,128)S(1)} %get-tuple-element.1523), channel_id=1, source_target_pairs={{1,0},{2,1},{3,2},{0,3},{5,4},{6,5},{7,6},{4,7},{9,8},{10,9},{11,1... | collective-permute-start | bytes 488 | tf_op jit(solution)/shard_map/ppermute | solution.py:32
  34.3 11.0 %copy-start.16 = (f32[5,8,8192]{2,1,0:T(8,128)S(1)}, f32[5,8,8192]{2,1,0:T(8,128)}, u32[]{:S(2)}) copy-start(f32[5,8,8192]{2,1,0:T(8,128)} %param.39) | copy-start | bytes 3932164
  45.2 1.3 copy-start.17
  46.6 3.1 copy-start.22
  98.6 2.6 copy-start.4
  101.2 8.1 copy-start.5
  101.2 7.6 collective-permute-start
  108.8 1.2 copy-start
  110.0 9.4 %copy-start.5 = (f32[5,8192]{1,0:T(8,128)S(1)}, f32[5,8192]{1,0:T(8,128)}, u32[]{:S(2)}) copy-start(f32[5,8192]{1,0:T(8,128)} %get-tuple-element.2013) | copy-start | bytes 491524 | tf_op jit(solution)/shard_map/while
  110.0 8.9 %collective-permute-start = (f32[5,8192]{1,0:T(8,128)}, f32[5,8192]{1,0:T(8,128)S(1)}, u32[]{:S(2)}, u32[]{:S(2)}) collective-permute-start(f32[5,8192]{1,0:T(8,128)} %get-tuple-element.2004), channel_id=1, source_target_pairs={{0,4},{4,8},{8,12},{12,16},{16,20},{20,24},{24,28},{1,5},{5,9},{9,... | collective-permute-start | bytes 491528 | tf_op jit(solution)/shard_map/while/body/eval_jaxpr/ppermute | solution.py:42
  118.9 1.2 copy-start
  120.1 9.4 %copy-start.5 = (f32[5,8192]{1,0:T(8,128)S(1)}, f32[5,8192]{1,0:T(8,128)}, u32[]{:S(2)}) copy-start(f32[5,8192]{1,0:T(8,128)} %get-tuple-element.2013) | copy-start | bytes 491524 | tf_op jit(solution)/shard_map/while
  120.1 8.9 %collective-permute-start = (f32[5,8192]{1,0:T(8,128)}, f32[5,8192]{1,0:T(8,128)S(1)}, u32[]{:S(2)}, u32[]{:S(2)}) collective-permute-start(f32[5,8192]{1,0:T(8,128)} %get-tuple-element.2004), channel_id=1, source_target_pairs={{0,4},{4,8},{8,12},{12,16},{16,20},{20,24},{24,28},{1,5},{5,9},{9,... | collective-permute-start | bytes 491528 | tf_op jit(solution)/shard_map/while/body/eval_jaxpr/ppermute | solution.py:42
  129.0 1.2 copy-start
  130.2 9.4 %copy-start.5 = (f32[5,8192]{1,0:T(8,128)S(1)}, f32[5,8192]{1,0:T(8,128)}, u32[]{:S(2)}) copy-start(f32[5,8192]{1,0:T(8,128)} %get-tuple-element.2013) | copy-start | bytes 491524 | tf_op jit(solution)/shard_map/while
  130.2 8.9 %collective-permute-start = (f32[5,8192]{1,0:T(8,128)}, f32[5,8192]{1,0:T(8,128)S(1)}, u32[]{:S(2)}, u32[]{:S(2)}) collective-permute-start(f32[5,8192]{1,0:T(8,128)} %get-tuple-element.2004), channel_id=1, source_target_pairs={{0,4},{4,8},{8,12},{12,16},{16,20},{20,24},{24,28},{1,5},{5,9},{9,... | collective-permute-start | bytes 491528 | tf_op jit(solution)/shard_map/while/body/eval_jaxpr/ppermute | solution.py:42
  139.1 1.2 copy-start
  140.3 9.4 %copy-start.5 = (f32[5,8192]{1,0:T(8,128)S(1)}, f32[5,8192]{1,0:T(8,128)}, u32[]{:S(2)}) copy-start(f32[5,8192]{1,0:T(8,128)} %get-tuple-element.2013) | copy-start | bytes 491524 | tf_op jit(solution)/shard_map/while
  140.3 8.9 %collective-permute-start = (f32[5,8192]{1,0:T(8,128)}, f32[5,8192]{1,0:T(8,128)S(1)}, u32[]{:S(2)}, u32[]{:S(2)}) collective-permute-start(f32[5,8192]{1,0:T(8,128)} %get-tuple-element.2004), channel_id=1, source_target_pairs={{0,4},{4,8},{8,12},{12,16},{16,20},{20,24},{24,28},{1,5},{5,9},{9,... | collective-permute-start | bytes 491528 | tf_op jit(solution)/shard_map/while/body/eval_jaxpr/ppermute | solution.py:42
  149.2 1.2 copy-start
  150.4 9.4 %copy-start.5 = (f32[5,8192]{1,0:T(8,128)S(1)}, f32[5,8192]{1,0:T(8,128)}, u32[]{:S(2)}) copy-start(f32[5,8192]{1,0:T(8,128)} %get-tuple-element.2013) | copy-start | bytes 491524 | tf_op jit(solution)/shard_map/while
  150.4 8.9 %collective-permute-start = (f32[5,8192]{1,0:T(8,128)}, f32[5,8192]{1,0:T(8,128)S(1)}, u32[]{:S(2)}, u32[]{:S(2)}) collective-permute-start(f32[5,8192]{1,0:T(8,128)} %get-tuple-element.2004), channel_id=1, source_target_pairs={{0,4},{4,8},{8,12},{12,16},{16,20},{20,24},{24,28},{1,5},{5,9},{9,... | collective-permute-start | bytes 491528 | tf_op jit(solution)/shard_map/while/body/eval_jaxpr/ppermute | solution.py:42
  160.5 9.4 %copy-start.5 = (f32[5,8192]{1,0:T(8,128)S(1)}, f32[5,8192]{1,0:T(8,128)}, u32[]{:S(2)}) copy-start(f32[5,8192]{1,0:T(8,128)} %get-tuple-element.2013) | copy-start | bytes 491524 | tf_op jit(solution)/shard_map/while
  160.5 8.9 %collective-permute-start = (f32[5,8192]{1,0:T(8,128)}, f32[5,8192]{1,0:T(8,128)S(1)}, u32[]{:S(2)}, u32[]{:S(2)}) collective-permute-start(f32[5,8192]{1,0:T(8,128)} %get-tuple-element.2004), channel_id=1, source_target_pairs={{0,4},{4,8},{8,12},{12,16},{16,20},{20,24},{24,28},{1,5},{5,9},{9,... | collective-permute-start | bytes 491528 | tf_op jit(solution)/shard_map/while/body/eval_jaxpr/ppermute | solution.py:42
  170.6 9.4 %copy-start.5 = (f32[5,8192]{1,0:T(8,128)S(1)}, f32[5,8192]{1,0:T(8,128)}, u32[]{:S(2)}) copy-start(f32[5,8192]{1,0:T(8,128)} %get-tuple-element.2013) | copy-start | bytes 491524 | tf_op jit(solution)/shard_map/while
  170.6 8.9 %collective-permute-start = (f32[5,8192]{1,0:T(8,128)}, f32[5,8192]{1,0:T(8,128)S(1)}, u32[]{:S(2)}, u32[]{:S(2)}) collective-permute-start(f32[5,8192]{1,0:T(8,128)} %get-tuple-element.2004), channel_id=1, source_target_pairs={{0,4},{4,8},{8,12},{12,16},{16,20},{20,24},{24,28},{1,5},{5,9},{9,... | collective-permute-start | bytes 491528 | tf_op jit(solution)/shard_map/while/body/eval_jaxpr/ppermute | solution.py:42
  269.9 9.4 %collective-permute-start.1 = (f32[5,8192]{1,0:T(8,128)}, f32[5,8192]{1,0:T(8,128)S(1)}, u32[]{:S(2)}, u32[]{:S(2)}) collective-permute-start(f32[5,8192]{1,0:T(8,128)} %get-tuple-element.2076), channel_id=1, source_target_pairs={{4,0},{8,4},{12,8},{16,12},{20,16},{24,20},{28,24},{5,1},{9,5},{13... | collective-permute-start | bytes 491528 | tf_op jit(solution)/shard_map/while/body/eval_jaxpr/ppermute | solution.py:42
  280.5 8.8 %collective-permute-start.1 = (f32[5,8192]{1,0:T(8,128)}, f32[5,8192]{1,0:T(8,128)S(1)}, u32[]{:S(2)}, u32[]{:S(2)}) collective-permute-start(f32[5,8192]{1,0:T(8,128)} %get-tuple-element.2076), channel_id=1, source_target_pairs={{4,0},{8,4},{12,8},{16,12},{20,16},{24,20},{28,24},{5,1},{9,5},{13... | collective-permute-start | bytes 491528 | tf_op jit(solution)/shard_map/while/body/eval_jaxpr/ppermute | solution.py:42
  290.5 8.8 %collective-permute-start.1 = (f32[5,8192]{1,0:T(8,128)}, f32[5,8192]{1,0:T(8,128)S(1)}, u32[]{:S(2)}, u32[]{:S(2)}) collective-permute-start(f32[5,8192]{1,0:T(8,128)} %get-tuple-element.2076), channel_id=1, source_target_pairs={{4,0},{8,4},{12,8},{16,12},{20,16},{24,20},{28,24},{5,1},{9,5},{13... | collective-permute-start | bytes 491528 | tf_op jit(solution)/shard_map/while/body/eval_jaxpr/ppermute | solution.py:42
  300.4 8.8 %collective-permute-start.1 = (f32[5,8192]{1,0:T(8,128)}, f32[5,8192]{1,0:T(8,128)S(1)}, u32[]{:S(2)}, u32[]{:S(2)}) collective-permute-start(f32[5,8192]{1,0:T(8,128)} %get-tuple-element.2076), channel_id=1, source_target_pairs={{4,0},{8,4},{12,8},{16,12},{20,16},{24,20},{28,24},{5,1},{9,5},{13... | collective-permute-start | bytes 491528 | tf_op jit(solution)/shard_map/while/body/eval_jaxpr/ppermute | solution.py:42
  310.4 8.8 %collective-permute-start.1 = (f32[5,8192]{1,0:T(8,128)}, f32[5,8192]{1,0:T(8,128)S(1)}, u32[]{:S(2)}, u32[]{:S(2)}) collective-permute-start(f32[5,8192]{1,0:T(8,128)} %get-tuple-element.2076), channel_id=1, source_target_pairs={{4,0},{8,4},{12,8},{16,12},{20,16},{24,20},{28,24},{5,1},{9,5},{13... | collective-permute-start | bytes 491528 | tf_op jit(solution)/shard_map/while/body/eval_jaxpr/ppermute | solution.py:42
  320.3 8.8 %collective-permute-start.1 = (f32[5,8192]{1,0:T(8,128)}, f32[5,8192]{1,0:T(8,128)S(1)}, u32[]{:S(2)}, u32[]{:S(2)}) collective-permute-start(f32[5,8192]{1,0:T(8,128)} %get-tuple-element.2076), channel_id=1, source_target_pairs={{4,0},{8,4},{12,8},{16,12},{20,16},{24,20},{28,24},{5,1},{9,5},{13... | collective-permute-start | bytes 491528 | tf_op jit(solution)/shard_map/while/body/eval_jaxpr/ppermute | solution.py:42
  330.3 8.8 %collective-permute-start.1 = (f32[5,8192]{1,0:T(8,128)}, f32[5,8192]{1,0:T(8,128)S(1)}, u32[]{:S(2)}, u32[]{:S(2)}) collective-permute-start(f32[5,8192]{1,0:T(8,128)} %get-tuple-element.2076), channel_id=1, source_target_pairs={{4,0},{8,4},{12,8},{16,12},{20,16},{24,20},{28,24},{5,1},{9,5},{13... | collective-permute-start | bytes 491528 | tf_op jit(solution)/shard_map/while/body/eval_jaxpr/ppermute | solution.py:42
  340.2 8.8 %collective-permute-start.1 = (f32[5,8192]{1,0:T(8,128)}, f32[5,8192]{1,0:T(8,128)S(1)}, u32[]{:S(2)}, u32[]{:S(2)}) collective-permute-start(f32[5,8192]{1,0:T(8,128)} %get-tuple-element.2076), channel_id=1, source_target_pairs={{4,0},{8,4},{12,8},{16,12},{20,16},{24,20},{28,24},{5,1},{9,5},{13... | collective-permute-start | bytes 491528 | tf_op jit(solution)/shard_map/while/body/eval_jaxpr/ppermute | solution.py:42
  351.3 82.2 %copy-start.12 = (f32[5,8,8192]{2,1,0:T(8,128)S(1)}, f32[5,8,8192]{2,1,0:T(8,128)}, u32[]{:S(2)}) copy-start(f32[5,8,8192]{2,1,0:T(8,128)} %param.36) | copy-start | bytes 3932164
  456.4 11.0 %all-to-all-start.1 = ((f32[32,5,2,128]{3,2,1,0:T(2,128)}), f32[32,5,2,128]{3,2,1,0:T(2,128)S(1)}, u32[]{:S(2)}, u32[]{:S(2)}) async-start(f32[32,5,2,128]{3,2,1,0:T(2,128)} %constant_dynamic-update-slice_fusion.32), calls=%async_computation.1 | async-start | bytes 327680 | tf_op jit(solution)/shard_map/all_to_all | solution.py:12
  459.4 11.9 %collective-permute-start.6 = (f32[5,8,1]{2,1,0:T(8,128)S(1)}, f32[5,8,1]{2,1,0:T(8,128)S(1)}, u32[]{:S(2)}, u32[]{:S(2)}) collective-permute-start(f32[5,8,1]{2,1,0:T(8,128)S(1)} %get-tuple-element.1520), channel_id=1, source_target_pairs={{0,1},{1,2},{2,3},{3,0},{4,5},{5,6},{6,7},{7,4},{8,9},{9,10},{10,1... | collective-permute-start | bytes 488 | tf_op jit(solution)/shard_map/ppermute | solution.py:30
  460.6 10.8 %collective-permute-start.7 = (f32[5,8,1]{2,1,0:T(8,128)S(1)}, f32[5,8,1]{2,1,0:T(8,128)S(1)}, u32[]{:S(2)}, u32[]{:S(2)}) collective-permute-start(f32[5,8,1]{2,1,0:T(8,128)S(1)} %get-tuple-element.1521), channel_id=1, source_target_pairs={{1,0},{2,1},{3,2},{0,3},{5,4},{6,5},{7,6},{4,7},{9,8},{10,9},{11,1... | collective-permute-start | bytes 488 | tf_op jit(solution)/shard_map/ppermute | solution.py:32
  469.7 1.6 copy-start.15
  469.7 1.6 copy-start.18
  515.2 7.1 collective-permute-start.2
  523.5 8.8 %collective-permute-start.2 = (f32[5,8192]{1,0:T(8,128)}, f32[5,8192]{1,0:T(8,128)S(1)}, u32[]{:S(2)}, u32[]{:S(2)}) collective-permute-start(f32[5,8192]{1,0:T(8,128)} %get-tuple-element.2145), channel_id=1, source_target_pairs={{0,4},{4,8},{8,12},{12,16},{16,20},{20,24},{24,28},{1,5},{5,9},{9,... | collective-permute-start | bytes 491528 | tf_op jit(solution)/shard_map/while/body/eval_jaxpr/ppermute | solution.py:42
  533.5 8.8 %collective-permute-start.2 = (f32[5,8192]{1,0:T(8,128)}, f32[5,8192]{1,0:T(8,128)S(1)}, u32[]{:S(2)}, u32[]{:S(2)}) collective-permute-start(f32[5,8192]{1,0:T(8,128)} %get-tuple-element.2145), channel_id=1, source_target_pairs={{0,4},{4,8},{8,12},{12,16},{16,20},{20,24},{24,28},{1,5},{5,9},{9,... | collective-permute-start | bytes 491528 | tf_op jit(solution)/shard_map/while/body/eval_jaxpr/ppermute | solution.py:42
  543.4 8.8 %collective-permute-start.2 = (f32[5,8192]{1,0:T(8,128)}, f32[5,8192]{1,0:T(8,128)S(1)}, u32[]{:S(2)}, u32[]{:S(2)}) collective-permute-start(f32[5,8192]{1,0:T(8,128)} %get-tuple-element.2145), channel_id=1, source_target_pairs={{0,4},{4,8},{8,12},{12,16},{16,20},{20,24},{24,28},{1,5},{5,9},{9,... | collective-permute-start | bytes 491528 | tf_op jit(solution)/shard_map/while/body/eval_jaxpr/ppermute | solution.py:42
  553.4 8.8 %collective-permute-start.2 = (f32[5,8192]{1,0:T(8,128)}, f32[5,8192]{1,0:T(8,128)S(1)}, u32[]{:S(2)}, u32[]{:S(2)}) collective-permute-start(f32[5,8192]{1,0:T(8,128)} %get-tuple-element.2145), channel_id=1, source_target_pairs={{0,4},{4,8},{8,12},{12,16},{16,20},{20,24},{24,28},{1,5},{5,9},{9,... | collective-permute-start | bytes 491528 | tf_op jit(solution)/shard_map/while/body/eval_jaxpr/ppermute | solution.py:42
  563.4 8.8 %collective-permute-start.2 = (f32[5,8192]{1,0:T(8,128)}, f32[5,8192]{1,0:T(8,128)S(1)}, u32[]{:S(2)}, u32[]{:S(2)}) collective-permute-start(f32[5,8192]{1,0:T(8,128)} %get-tuple-element.2145), channel_id=1, source_target_pairs={{0,4},{4,8},{8,12},{12,16},{16,20},{20,24},{24,28},{1,5},{5,9},{9,... | collective-permute-start | bytes 491528 | tf_op jit(solution)/shard_map/while/body/eval_jaxpr/ppermute | solution.py:42
  573.3 8.8 %collective-permute-start.2 = (f32[5,8192]{1,0:T(8,128)}, f32[5,8192]{1,0:T(8,128)S(1)}, u32[]{:S(2)}, u32[]{:S(2)}) collective-permute-start(f32[5,8192]{1,0:T(8,128)} %get-tuple-element.2145), channel_id=1, source_target_pairs={{0,4},{4,8},{8,12},{12,16},{16,20},{20,24},{24,28},{1,5},{5,9},{9,... | collective-permute-start | bytes 491528 | tf_op jit(solution)/shard_map/while/body/eval_jaxpr/ppermute | solution.py:42
  583.3 8.8 %collective-permute-start.2 = (f32[5,8192]{1,0:T(8,128)}, f32[5,8192]{1,0:T(8,128)S(1)}, u32[]{:S(2)}, u32[]{:S(2)}) collective-permute-start(f32[5,8192]{1,0:T(8,128)} %get-tuple-element.2145), channel_id=1, source_target_pairs={{0,4},{4,8},{8,12},{12,16},{16,20},{20,24},{24,28},{1,5},{5,9},{9,... | collective-permute-start | bytes 491528 | tf_op jit(solution)/shard_map/while/body/eval_jaxpr/ppermute | solution.py:42
  693.0 9.4 %collective-permute-start.3 = (f32[5,8192]{1,0:T(8,128)}, f32[5,8192]{1,0:T(8,128)S(1)}, u32[]{:S(2)}, u32[]{:S(2)}) collective-permute-start(f32[5,8192]{1,0:T(8,128)} %get-tuple-element.2217), channel_id=1, source_target_pairs={{4,0},{8,4},{12,8},{16,12},{20,16},{24,20},{28,24},{5,1},{9,5},{13... | collective-permute-start | bytes 491528 | tf_op jit(solution)/shard_map/while/body/eval_jaxpr/ppermute | solution.py:42
  703.6 8.8 %collective-permute-start.3 = (f32[5,8192]{1,0:T(8,128)}, f32[5,8192]{1,0:T(8,128)S(1)}, u32[]{:S(2)}, u32[]{:S(2)}) collective-permute-start(f32[5,8192]{1,0:T(8,128)} %get-tuple-element.2217), channel_id=1, source_target_pairs={{4,0},{8,4},{12,8},{16,12},{20,16},{24,20},{28,24},{5,1},{9,5},{13... | collective-permute-start | bytes 491528 | tf_op jit(solution)/shard_map/while/body/eval_jaxpr/ppermute | solution.py:42
  713.6 8.8 %collective-permute-start.3 = (f32[5,8192]{1,0:T(8,128)}, f32[5,8192]{1,0:T(8,128)S(1)}, u32[]{:S(2)}, u32[]{:S(2)}) collective-permute-start(f32[5,8192]{1,0:T(8,128)} %get-tuple-element.2217), channel_id=1, source_target_pairs={{4,0},{8,4},{12,8},{16,12},{20,16},{24,20},{28,24},{5,1},{9,5},{13... | collective-permute-start | bytes 491528 | tf_op jit(solution)/shard_map/while/body/eval_jaxpr/ppermute | solution.py:42
  723.5 8.8 %collective-permute-start.3 = (f32[5,8192]{1,0:T(8,128)}, f32[5,8192]{1,0:T(8,128)S(1)}, u32[]{:S(2)}, u32[]{:S(2)}) collective-permute-start(f32[5,8192]{1,0:T(8,128)} %get-tuple-element.2217), channel_id=1, source_target_pairs={{4,0},{8,4},{12,8},{16,12},{20,16},{24,20},{28,24},{5,1},{9,5},{13... | collective-permute-start | bytes 491528 | tf_op jit(solution)/shard_map/while/body/eval_jaxpr/ppermute | solution.py:42
  733.5 8.8 %collective-permute-start.3 = (f32[5,8192]{1,0:T(8,128)}, f32[5,8192]{1,0:T(8,128)S(1)}, u32[]{:S(2)}, u32[]{:S(2)}) collective-permute-start(f32[5,8192]{1,0:T(8,128)} %get-tuple-element.2217), channel_id=1, source_target_pairs={{4,0},{8,4},{12,8},{16,12},{20,16},{24,20},{28,24},{5,1},{9,5},{13... | collective-permute-start | bytes 491528 | tf_op jit(solution)/shard_map/while/body/eval_jaxpr/ppermute | solution.py:42
  743.4 8.8 %collective-permute-start.3 = (f32[5,8192]{1,0:T(8,128)}, f32[5,8192]{1,0:T(8,128)S(1)}, u32[]{:S(2)}, u32[]{:S(2)}) collective-permute-start(f32[5,8192]{1,0:T(8,128)} %get-tuple-element.2217), channel_id=1, source_target_pairs={{4,0},{8,4},{12,8},{16,12},{20,16},{24,20},{28,24},{5,1},{9,5},{13... | collective-permute-start | bytes 491528 | tf_op jit(solution)/shard_map/while/body/eval_jaxpr/ppermute | solution.py:42
  753.4 8.8 %collective-permute-start.3 = (f32[5,8192]{1,0:T(8,128)}, f32[5,8192]{1,0:T(8,128)S(1)}, u32[]{:S(2)}, u32[]{:S(2)}) collective-permute-start(f32[5,8192]{1,0:T(8,128)} %get-tuple-element.2217), channel_id=1, source_target_pairs={{4,0},{8,4},{12,8},{16,12},{20,16},{24,20},{28,24},{5,1},{9,5},{13... | collective-permute-start | bytes 491528 | tf_op jit(solution)/shard_map/while/body/eval_jaxpr/ppermute | solution.py:42
  763.3 8.8 %collective-permute-start.3 = (f32[5,8192]{1,0:T(8,128)}, f32[5,8192]{1,0:T(8,128)S(1)}, u32[]{:S(2)}, u32[]{:S(2)}) collective-permute-start(f32[5,8192]{1,0:T(8,128)} %get-tuple-element.2217), channel_id=1, source_target_pairs={{4,0},{8,4},{12,8},{16,12},{20,16},{24,20},{28,24},{5,1},{9,5},{13... | collective-permute-start | bytes 491528 | tf_op jit(solution)/shard_map/while/body/eval_jaxpr/ppermute | solution.py:42
  840.1 1.5 copy-start.14
  (34 other events, 38.4 us)
